TPU v7x, 32 devices: a whole 2x2x4 slice. The times are simulated.
32 devices in a mesh: rep: 4 (over x, core), shard: 8 (over z, y).
Axes of the slice: x: 2, y: 2, z: 4, core: 2. Of those that a mesh axis runs over, the one named last changes fastest.
Arguments:
- hidden_in: bfloat16 [4, 4096, 896], P('rep', 'shard'), may hold values from -6 to 6
- cotangent: bfloat16 [4, 4096, 896], P('rep', 'shard'), may hold values from -6 to 6
- norm_gains: bfloat16 [2, 896], P(None, 'shard'), may hold values from 0.5 to 1.5
- q_bias: bfloat16 [896], P('shard'), may hold values from -3 to 3
- kv_bias: bfloat16 [256], P('shard'), may hold values from -3 to 3
- q_weight: bfloat16 [896, 896], P('shard'), may hold values from -0.1875 to 0.1875
- kv_weight: bfloat16 [896, 256], P('shard'), may hold values from -0.1875 to 0.1875
- out_weight: bfloat16 [896, 896], P('shard'), may hold values from -1.5 to 1.5
- gate_weight: bfloat16 [896, 4864], P('shard'), may hold values from -0.1875 to 0.1875
- up_weight: bfloat16 [896, 4864], P('shard'), may hold values from -0.1875 to 0.1875
- down_weight: bfloat16 [896, 4864], P('shard'), may hold values from -0.078125 to 0.078125
Outputs:
- output: bfloat16 [4, 4096, 896], P('rep', 'shard')
- input_grad: bfloat16 [4, 4096, 896], P('rep', 'shard')
- gains_grad: float32 [2, 896], P(None, 'shard')
- q_bias_grad: float32 [896], P('shard')
- kv_bias_grad: float32 [256], P('shard')
- q_weight_grad: float32 [896, 896], P('shard')
- kv_weight_grad: float32 [896, 256], P('shard')
- out_weight_grad: float32 [896, 896], P('shard')
- gate_weight_grad: float32 [896, 4864], P('shard')
- up_weight_grad: float32 [896, 4864], P('shard')
- down_weight_grad: float32 [896, 4864], P('shard')
All inputs are finite; a program needn't handle non-finite values.
Results may differ from a plain program's by a relative error of at most 0.02.
Values may be sent and summed in bfloat16 or wider, within the bound.
No kernel may reach another device: no remote copies, remote signals or barrier semaphores. Data moves between devices by JAX's collectives and lax.ppermute only.
A program may use at most 192 MiB of HBM per device.

v0:
```python
import math

import jax
import jax.numpy as jnp
from jax import lax
from jax.sharding import PartitionSpec as P

D = 896
HEADS = 14
KV_HEADS = 2
HEAD = 64
FF = 4864
QW = 896
KW = 128
KEY_BLOCK = 512


EPS = 1e-06
ROPE_BASE = 1000000.0


def rope_tables(positions, head_width):
    half_width = head_width // 2
    inverse = jnp.exp(
        jnp.arange(half_width, dtype=jnp.float32) * (-2.0 * math.log(ROPE_BASE) / head_width)
    )
    angles = positions.astype(jnp.float32)[:, None] * inverse[None, :]
    angles = jnp.concatenate([angles, angles], axis=1)
    return (jnp.cos(angles), jnp.sin(angles))


def rotate(source, cosine, sine):
    half_width = source.shape[-1] // 2
    turned = jnp.concatenate([-source[..., half_width:], source[..., :half_width]], axis=-1)
    return source * cosine[:, None, :] + turned * sine[:, None, :]


def rotate_back(source, cosine, sine):
    half_width = source.shape[-1] // 2
    scaled = source * sine[:, None, :]
    turned = jnp.concatenate([scaled[..., half_width:], -scaled[..., :half_width]], axis=-1)
    return source * cosine[:, None, :] + turned


def block_scores(q_group, kv_whole, column, step_index, positions):
    offset = step_index * KEY_BLOCK
    keys_block = lax.dynamic_slice(kv_whole, (offset, column), (KEY_BLOCK, HEAD))
    scores = jnp.einsum(
        "njd,kd->njk", q_group, keys_block, preferred_element_type=jnp.float32
    ) * HEAD ** (-0.5)
    key_pos = offset + jnp.arange(KEY_BLOCK, dtype=jnp.int32)
    allowed = key_pos[None, :] <= positions[:, None]
    return jnp.where(allowed[:, None, :], scores, -jnp.inf)


def norm_back(grad_normed, normed, inv_scale, gain_row):
    scaled = grad_normed * gain_row
    return inv_scale * (scaled - normed * jnp.mean(scaled * normed, axis=1, keepdims=True))


def outer_sum(left, right):
    return jnp.einsum("nr,nc->rc", left, right, preferred_element_type=jnp.float32)


def body(
    hidden_in,
    cotangent,
    norm_gains,
    q_bias,
    kv_bias,
    q_weight,
    kv_weight,
    out_weight,
    gate_weight,
    up_weight,
    down_weight,
):
    tok_rows = hidden_in.shape[1]
    shard_count = lax.axis_size("shard")
    shard_place = lax.axis_index("shard")
    row_share = D // shard_count
    group = HEADS // KV_HEADS
    scale = HEAD ** (-0.5)
    gain_rows, q_bias_all, kv_bias_all, q_full, kv_full = (
        lax.all_gather(norm_gains, "shard", axis=1, tiled=True),
        lax.all_gather(q_bias, "shard", axis=0, tiled=True),
        lax.all_gather(kv_bias, "shard", axis=0, tiled=True),
        lax.all_gather(q_weight, "shard", axis=0, tiled=True),
        lax.all_gather(kv_weight, "shard", axis=0, tiled=True),
    )
    gain_one = gain_rows[0].astype(jnp.float32)
    gain_two = gain_rows[1].astype(jnp.float32)
    inputs = hidden_in[0].astype(jnp.float32)
    inv_one = lax.rsqrt(jnp.mean(inputs * inputs, axis=1, keepdims=True) + EPS)
    normed_one = inputs * inv_one
    h_one = (normed_one * gain_one).astype(jnp.bfloat16)
    queries = jnp.dot(h_one, q_full, preferred_element_type=jnp.float32) + q_bias_all.astype(
        jnp.float32
    )
    keyvals = jnp.dot(h_one, kv_full, preferred_element_type=jnp.float32) + kv_bias_all.astype(
        jnp.float32
    )
    positions = shard_place * tok_rows + jnp.arange(tok_rows, dtype=jnp.int32)
    cosine, sine = rope_tables(positions, HEAD)
    q_heads = rotate(queries.reshape(tok_rows, HEADS, HEAD), cosine, sine).astype(jnp.bfloat16)
    k_rot = rotate(keyvals[:, :KW].reshape(tok_rows, KV_HEADS, HEAD), cosine, sine).reshape(
        tok_rows, KW
    )
    kv_local = jnp.concatenate([k_rot, keyvals[:, KW:]], axis=1).astype(jnp.bfloat16)
    kv_whole = lax.all_gather(kv_local, "shard", axis=0, tiled=True)
    needed = ((shard_place + 1) * tok_rows + KEY_BLOCK - 1) // KEY_BLOCK
    heads_out = []
    log_totals = []
    for g_index in range(KV_HEADS):
        q_group = q_heads[:, g_index * group : (g_index + 1) * group, :]

        def stats_step(step_index, running):
            run_max, run_sum = running
            scores = block_scores(q_group, kv_whole, g_index * HEAD, step_index, positions)
            new_max = jnp.maximum(run_max, jnp.max(scores, axis=2))
            run_sum = run_sum * jnp.exp(run_max - new_max) + jnp.sum(
                jnp.exp(scores - new_max[:, :, None]), axis=2
            )
            return (new_max, run_sum)

        start_max = jnp.full((tok_rows, group), -jnp.inf, jnp.float32)
        run_max, run_sum = lax.fori_loop(
            0, needed, stats_step, (start_max, jnp.zeros((tok_rows, group), jnp.float32))
        )
        log_total = run_max + jnp.log(run_sum)

        def value_step(step_index, running):
            scores = block_scores(q_group, kv_whole, g_index * HEAD, step_index, positions)
            probab = jnp.exp(scores - log_total[:, :, None]).astype(jnp.bfloat16)
            values_block = lax.dynamic_slice(
                kv_whole, (step_index * KEY_BLOCK, KW + g_index * HEAD), (KEY_BLOCK, HEAD)
            )
            return running + jnp.einsum(
                "njk,kd->njd", probab, values_block, preferred_element_type=jnp.float32
            )

        attended = lax.fori_loop(
            0, needed, value_step, jnp.zeros((tok_rows, group, HEAD), jnp.float32)
        )
        heads_out.append(attended.astype(jnp.bfloat16))
        log_totals.append(log_total)
    attn_b = jnp.concatenate(heads_out, axis=1).reshape(tok_rows, QW)
    out_full = lax.all_gather(out_weight, "shard", axis=0, tiled=True)
    middle = inputs + jnp.dot(attn_b, out_full.T, preferred_element_type=jnp.float32)
    inv_two = lax.rsqrt(jnp.mean(middle * middle, axis=1, keepdims=True) + EPS)
    normed_two = middle * inv_two
    h_two = (normed_two * gain_two).astype(jnp.bfloat16)
    gate_full, up_full, down_full = (
        lax.all_gather(gate_weight, "shard", axis=0, tiled=True),
        lax.all_gather(up_weight, "shard", axis=0, tiled=True),
        lax.all_gather(down_weight, "shard", axis=0, tiled=True),
    )
    gate_lin = jnp.dot(h_two, gate_full, preferred_element_type=jnp.float32)
    up_lin = jnp.dot(h_two, up_full, preferred_element_type=jnp.float32)
    sigmoid_gate = jax.nn.sigmoid(gate_lin)
    silu_gate = gate_lin * sigmoid_gate
    hidden_b = (silu_gate * up_lin).astype(jnp.bfloat16)
    output = middle + jnp.dot(hidden_b, down_full.T, preferred_element_type=jnp.float32)
    grad_out = cotangent[0]
    grad_hidden = jnp.dot(
        grad_out,
        lax.all_gather(down_weight, "shard", axis=0, tiled=True),
        preferred_element_type=jnp.float32,
    )
    grad_gate_b = (
        grad_hidden * up_lin * sigmoid_gate * (1.0 + gate_lin * (1.0 - sigmoid_gate))
    ).astype(jnp.bfloat16)
    grad_up_b = (grad_hidden * silu_gate).astype(jnp.bfloat16)
    portions = lax.all_gather((gate_weight, up_weight), "shard", axis=0, tiled=True)
    grad_h_two = jnp.dot(grad_gate_b, portions[0].T, preferred_element_type=jnp.float32) + jnp.dot(
        grad_up_b, portions[1].T, preferred_element_type=jnp.float32
    )
    gain_two_grad = jnp.sum(grad_h_two * normed_two, axis=0)
    grad_middle = grad_out.astype(jnp.float32) + norm_back(
        grad_h_two, normed_two, inv_two, gain_two
    )
    grad_branch_b = grad_middle.astype(jnp.bfloat16)
    grad_attn = jnp.dot(
        grad_branch_b,
        lax.all_gather(out_weight, "shard", axis=0, tiled=True),
        preferred_element_type=jnp.float32,
    )
    grad_heads = grad_attn.astype(jnp.bfloat16).reshape(tok_rows, HEADS, HEAD)
    grad_queries = []
    grad_keyvals = jnp.zeros((kv_whole.shape[0], 2 * KW), jnp.float32)
    for g_index in range(KV_HEADS):
        q_group = q_heads[:, g_index * group : (g_index + 1) * group, :]
        do_group = grad_heads[:, g_index * group : (g_index + 1) * group, :]
        log_total = log_totals[g_index]

        def probs_grads(step_index):
            scores = block_scores(q_group, kv_whole, g_index * HEAD, step_index, positions)
            probab = jnp.exp(scores - log_total[:, :, None])
            values_block = lax.dynamic_slice(
                kv_whole, (step_index * KEY_BLOCK, KW + g_index * HEAD), (KEY_BLOCK, HEAD)
            )
            grad_probab = jnp.einsum(
                "njd,kd->njk", do_group, values_block, preferred_element_type=jnp.float32
            )
            return (probab, grad_probab)

        def delta_step(step_index, running):
            probab, grad_probab = probs_grads(step_index)
            return running + jnp.sum(probab * grad_probab, axis=2)

        delta = lax.fori_loop(0, needed, delta_step, jnp.zeros((tok_rows, group), jnp.float32))

        def grad_step(step_index, running):
            grad_query, grad_kv = running
            probab, grad_probab = probs_grads(step_index)
            offset = step_index * KEY_BLOCK
            keys_block = lax.dynamic_slice(kv_whole, (offset, g_index * HEAD), (KEY_BLOCK, HEAD))
            grad_scores = (probab * (grad_probab - delta[:, :, None])).astype(jnp.bfloat16)
            grad_query = (
                grad_query
                + jnp.einsum(
                    "njk,kd->njd", grad_scores, keys_block, preferred_element_type=jnp.float32
                )
                * scale
            )
            grad_keys = (
                jnp.einsum("njk,njd->kd", grad_scores, q_group, preferred_element_type=jnp.float32)
                * scale
            )
            grad_values = jnp.einsum(
                "njk,njd->kd",
                probab.astype(jnp.bfloat16),
                do_group,
                preferred_element_type=jnp.float32,
            )
            old_keys = lax.dynamic_slice(grad_kv, (offset, g_index * HEAD), (KEY_BLOCK, HEAD))
            grad_kv = lax.dynamic_update_slice(
                grad_kv, old_keys + grad_keys, (offset, g_index * HEAD)
            )
            old_values = lax.dynamic_slice(
                grad_kv, (offset, KW + g_index * HEAD), (KEY_BLOCK, HEAD)
            )
            grad_kv = lax.dynamic_update_slice(
                grad_kv, old_values + grad_values, (offset, KW + g_index * HEAD)
            )
            return (grad_query, grad_kv)

        grad_query, grad_keyvals = lax.fori_loop(
            0, needed, grad_step, (jnp.zeros((tok_rows, group, HEAD), jnp.float32), grad_keyvals)
        )
        grad_queries.append(grad_query)
    grad_kv_mine = lax.psum_scatter(
        grad_keyvals.astype(jnp.bfloat16), "shard", scatter_dimension=0, tiled=True
    ).astype(jnp.float32)
    grad_q_rot = jnp.concatenate(grad_queries, axis=1)
    grad_q_b = rotate_back(grad_q_rot, cosine, sine).reshape(tok_rows, QW).astype(jnp.bfloat16)
    grad_k_lin = rotate_back(
        grad_kv_mine[:, :KW].reshape(tok_rows, KV_HEADS, HEAD), cosine, sine
    ).reshape(tok_rows, KW)
    grad_kv_b = jnp.concatenate([grad_k_lin, grad_kv_mine[:, KW:]], axis=1).astype(jnp.bfloat16)
    q_bias_sum = jnp.sum(grad_q_b.astype(jnp.float32), axis=0)
    kv_bias_sum = jnp.sum(grad_kv_b.astype(jnp.float32), axis=0)
    portions = lax.all_gather((q_weight, kv_weight), "shard", axis=0, tiled=True)
    grad_h_one = jnp.dot(grad_q_b, portions[0].T, preferred_element_type=jnp.float32) + jnp.dot(
        grad_kv_b, portions[1].T, preferred_element_type=jnp.float32
    )
    gain_one_grad = jnp.sum(grad_h_one * normed_one, axis=0)
    input_grad = (grad_middle + norm_back(grad_h_one, normed_one, inv_one, gain_one)).astype(
        jnp.bfloat16
    )
    group_sums = lax.psum_scatter(
        jnp.concatenate(
            [
                jnp.concatenate([outer_sum(h_one, grad_q_b), outer_sum(h_one, grad_kv_b)], axis=1),
                jnp.concatenate(
                    [
                        outer_sum(grad_branch_b, attn_b),
                        outer_sum(h_two, grad_gate_b),
                        outer_sum(h_two, grad_up_b),
                        outer_sum(grad_out, hidden_b),
                    ],
                    axis=1,
                ),
            ],
            axis=1,
        ).astype(jnp.bfloat16),
        "shard",
        scatter_dimension=0,
        tiled=True,
    )
    weight_sums = lax.psum(group_sums, "rep").astype(jnp.float32)
    gains_full, q_bias_full, kv_bias_full = lax.psum(
        (jnp.stack([gain_one_grad, gain_two_grad], axis=0), q_bias_sum, kv_bias_sum),
        ("rep", "shard"),
    )
    gains_grad = lax.dynamic_slice_in_dim(gains_full, shard_place * row_share, row_share, 1)
    q_bias_grad = lax.dynamic_slice_in_dim(
        q_bias_full, shard_place * (QW // shard_count), QW // shard_count, 0
    )
    kv_bias_grad = lax.dynamic_slice_in_dim(
        kv_bias_full, shard_place * (2 * KW // shard_count), 2 * KW // shard_count, 0
    )
    edges = [
        0,
        QW,
        QW + 2 * KW,
        2 * QW + 2 * KW,
        2 * QW + 2 * KW + FF,
        2 * QW + 2 * KW + 2 * FF,
        2 * QW + 2 * KW + 3 * FF,
    ]
    pieces = [
        weight_sums[:, edges[place_index] : edges[place_index + 1]] for place_index in range(6)
    ]
    return (
        output.astype(jnp.bfloat16)[None],
        input_grad[None],
        gains_grad,
        q_bias_grad,
        kv_bias_grad,
        pieces[0],
        pieces[1],
        pieces[2],
        pieces[3],
        pieces[4],
        pieces[5],
    )


def solution(mesh):
    placed = (
        P("rep", "shard", None),
        P("rep", "shard", None),
        P(None, "shard"),
        P("shard"),
        P("shard"),
        P("shard", None),
        P("shard", None),
        P("shard", None),
        P("shard", None),
        P("shard", None),
        P("shard", None),
    )
    return jax.shard_map(
        body,
        mesh=mesh,
        in_specs=placed,
        out_specs=(
            P("rep", "shard", None),
            P("rep", "shard", None),
            P(None, "shard"),
            P("shard"),
            P("shard"),
            P("shard", None),
            P("shard", None),
            P("shard", None),
            P("shard", None),
            P("shard", None),
            P("shard", None),
        ),
        check_vma=False,
    )
```

profile of v0, /device:TPU:0, one launch (start us, length us, event | category | flops | bytes accessed | tf_op | source)
XLA Modules:
  0.0 1598.0 jit_solution(14523239423939685275)
XLA Ops:
  12.2 23.2 %all-reduce.3 = (bf16[256]{0:T(256)(128)(2,1)S(1)}, bf16[896]{0:T(1024)(128)(2,1)S(1)}) all-reduce(bf16[256]{0:T(256)(128)(2,1)S(1)} %dynamic-update-slice, bf16[896]{0:T(1024)(128)(2,1)S(1)} %dynamic-update-slice.1), channel_id=1, replica_groups=mesh['rep'=4,'shard'=8] {'shard'}, use_global_device_ids=true, to_apply=%add | all-reduce | flops 1152 | bytes 4608
  35.4 16.5 %all-gather = bf16[8,112,2]{1,2,0:T(2,128)(2,1)S(1)} all-gather(bf16[1,112,2]{1,2,0:T(2,128)(2,1)} %bitcast.431), channel_id=1, replica_groups=mesh['rep'=4,'shard'=8] {'shard'}, dimensions={0}, use_global_device_ids=true | all-gather | bytes 4032 | tf_op jit(solution)/shard_map/all_gather | solution.py:85
  53.4 31.3 %all_gather.37 = bf16[896,256]{1,0:T(8,128)(2,1)S(1)} all-gather(bf16[112,256]{1,0:T(8,128)(2,1)} %param.33), channel_id=1, replica_groups=mesh['rep'=4,'shard'=8] {'shard'}, dimensions={0}, use_global_device_ids=true | all-gather | bytes 516096 | tf_op jit(solution)/shard_map/all_gather | solution.py:89
  97.2 40.8 %all-gather.8.cloned.1.call-done = bf16[4096,256]{0,1:T(8,128)(2,1)} async-done(((bf16[512,256]{0,1:T(8,128)(2,1)}), bf16[4096,256]{0,1:T(8,128)(2,1)}) %all-gather.8.cloned.1.call-update) | async-done | bytes 2097168 | tf_op jit(solution)/shard_map/all_gather | solution.py:110
  155.5 27.1 %all-gather.12.cloned.1.call-done = bf16[896,896]{1,0:T(8,128)(2,1)} async-done(((bf16[112,896]{1,0:T(8,128)(2,1)}), bf16[896,896]{1,0:T(8,128)(2,1)}) %all-gather.12.cloned.1.call-update) | async-done | bytes 1605648 | tf_op jit(solution)/shard_map/all_gather | solution.py:148
  187.0 125.9 %all-gather.16.cloned.1.call-done = bf16[896,4864]{1,0:T(8,128)(2,1)} async-done(((bf16[112,4864]{1,0:T(8,128)(2,1)}), bf16[896,4864]{1,0:T(8,128)(2,1)}) %all-gather.16.cloned.1.call-update) | async-done | bytes 8716304 | tf_op jit(solution)/shard_map/all_gather | solution.py:155
  312.9 11.6 fusion.209
  324.4 117.9 %all-gather.14.cloned.1.call-done = bf16[896,4864]{1,0:T(8,128)(2,1)} async-done(((bf16[112,4864]{1,0:T(8,128)(2,1)}), bf16[896,4864]{1,0:T(8,128)(2,1)}) %all-gather.14.cloned.1.call-update) | async-done | bytes 8716304 | tf_op jit(solution)/shard_map/all_gather | solution.py:154
  442.4 11.2 fusion.208
  453.6 118.3 %all-gather.18.cloned.1.call-done = bf16[896,4864]{1,0:T(8,128)(2,1)} async-done(((bf16[112,4864]{1,0:T(8,128)(2,1)}), bf16[896,4864]{1,0:T(8,128)(2,1)}) %all-gather.18.cloned.1.call-update) | async-done | bytes 8716304 | tf_op jit(solution)/shard_map/all_gather | solution.py:156
  571.9 17.1 %multiply_convert_fusion = (bf16[512,4864]{1,0:T(8,128)(2,1)}, bf16[512,4864]{1,0:T(8,128)(2,1)}, bf16[512,4864]{1,0:T(8,128)(2,1)}) fusion(f32[512,4864]{1,0:T(8,128)} %fusion.208, f32[512,4864]{1,0:T(8,128)} %fusion.209, bf16[896,4864]{1,0:T(8,128)(2,1)} %all-gather.18.cloned.1.call-done, bf16[1,512,896]{2,1,0:T(8,128)(2,1)S(1)} %copy-done.12), kind=kOutput, calls=%fused_computation.162 | convolution fusion | flops 4500094976 | bytes 44498944 | tf_op jit(solution)/shard_map/dot_general | solution.py:165
  589.1 12.0 fusion.210
  601.1 11.8 multiply_reduce_fusion
  623.4 5.8 while.100
  631.8 13.6 while.101
  645.6 13.6 while.103
  679.9 315.2 %reduce-scatter.3.cloned.1.call-done = bf16[512,256]{0,1:T(8,128)(2,1)} async-done(((bf16[4096,256]{0,1:T(8,128)(2,1)}), bf16[512,256]{0,1:T(8,128)(2,1)}) %reduce-scatter.3.cloned.1.call-update) | async-done | bytes 262160 | tf_op jit(solution)/shard_map/reduce_scatter | solution.py:252
  1001.8 10.8 fusion.156
  1012.6 10.8 fusion.155
  1023.4 7.6 bitcast_dynamic-update-slice_fusion
  1031.0 471.0 %reduce-scatter.5.cloned.1.call-done = bf16[112,16640]{1,0:T(8,128)(2,1)} async-done(((bf16[896,16640]{1,0:T(8,128)(2,1)}), bf16[112,16640]{1,0:T(8,128)(2,1)}) %reduce-scatter.5.cloned.1.call-update) | async-done | bytes 3727376 | tf_op jit(solution)/shard_map/reduce_scatter | solution.py:271
  1502.1 10.6 fusion.177
  1516.9 40.4 %all-reduce.2 = (f32[2,896]{1,0:T(2,128)S(1)}, f32[896]{0:T(1024)S(1)}, f32[256]{0:T(256)S(1)}) all-reduce(f32[2,896]{1,0:T(2,128)S(1)} %pad_maximum_fusion.7, f32[896]{0:T(1024)S(1)} %reduce_sum.117, f32[256]{0:T(256)S(1)} %convert_reduce_fusion.1), channel_id=1, replica_groups=mesh['rep'=4,'shard'=8] {'rep','shard'}, use_global_device_ids=true, to_apply=%region_29.30 | all-reduce | flops 2944 | bytes 23552 | tf_op jit(solution)/shard_map/psum | solution.py:292
  1562.0 20.9 %all-reduce.6.cloned.1.call-done = bf16[112,16640]{1,0:T(8,128)(2,1)} async-done(((bf16[112,16640]{1,0:T(8,128)(2,1)}), bf16[112,16640]{1,0:T(8,128)(2,1)}) %all-reduce.6.cloned.1.call-update) | async-done | bytes 3727376 | tf_op jit(solution)/shard_map/psum | solution.py:291
  (210 shorter events, 149.6 us)
Async XLA Ops:
  7.2 83.4 %all-gather.10.cloned.1.call-start = ((), (), s32[]{:S(2)}) async-start(), calls=%async_computation.3 | async-start | bytes 1806336 | tf_op jit(solution)/shard_map/all_gather | solution.py:88
  7.9 130.1 %all-gather.8.cloned.1.call-start = ((), (), s32[]{:S(2)}) async-start(), calls=%async_computation.2 | async-start | bytes 2359296 | tf_op jit(solution)/shard_map/all_gather | solution.py:110
  52.0 38.6 %copy-start.18 = (f32[896]{0:T(1024)}, f32[896]{0:T(1024)S(1)}, u32[]{:S(2)}) copy-start(f32[896]{0:T(1024)S(1)} %get-tuple-element.564) | copy-start | bytes 10756
  84.7 5.9 copy-start.20
  87.1 9.5 copy-start.6
  87.1 9.5 copy-start.8
  88.0 94.7 %all-gather.12.cloned.1.call-start = ((), (), s32[]{:S(2)}) async-start(), calls=%async_computation.4 | async-start | bytes 1806336 | tf_op jit(solution)/shard_map/all_gather | solution.py:148
  88.7 224.1 %all-gather.16.cloned.1.call-start = ((), (), s32[]{:S(2)}) async-start(), calls=%async_computation.6 | async-start | bytes 9805824 | tf_op jit(solution)/shard_map/all_gather | solution.py:155
  89.3 353.1 %all-gather.14.cloned.1.call-start = ((), (), s32[]{:S(2)}) async-start(), calls=%async_computation.5 | async-start | bytes 9805824 | tf_op jit(solution)/shard_map/all_gather | solution.py:154
  89.9 482.0 %all-gather.18.cloned.1.call-start = ((), (), s32[]{:S(2)}) async-start(), calls=%async_computation.7 | async-start | bytes 9805824 | tf_op jit(solution)/shard_map/all_gather | solution.py:156
  90.5 904.6 %reduce-scatter.3.cloned.1.call-start = ((), (), s32[]{:S(2)}) async-start(), calls=%async_computation.8 | async-start | bytes 2359296 | tf_op jit(solution)/shard_map/reduce_scatter | solution.py:252
  155.5 30.0 %copy-start.15 = (bf16[512,14,64]{0,2,1:T(8,128)(2,1)}, bf16[512,14,64]{0,2,1:T(8,128)(2,1)S(1)}, u32[]{:S(2)}) copy-start(bf16[512,14,64]{0,2,1:T(8,128)(2,1)S(1)} %pad_maximum_fusion) | copy-start | bytes 2752516
  186.9 255.4 %copy-start.16 = (bf16[512,896]{1,0:T(8,128)(2,1)}, bf16[512,896]{1,0:T(8,128)(2,1)S(1)}, u32[]{:S(2)}) copy-start(bf16[512,896]{1,0:T(8,128)(2,1)S(1)} %multiply_convert_fusion.3) | copy-start | bytes 2752516
  324.4 247.5 %copy-start.12 = (bf16[1,512,896]{2,1,0:T(8,128)(2,1)S(1)}, bf16[1,512,896]{2,1,0:T(8,128)(2,1)}, u32[]{:S(2)}) copy-start(bf16[1,512,896]{2,1,0:T(8,128)(2,1)} %param.28) | copy-start | bytes 2752516
  589.0 12.0 copy-start.3
  589.1 12.0 copy-start.24
  663.0 839.1 %reduce-scatter.5.cloned.1.call-start = ((), (), s32[]{:S(2)}) async-start(), calls=%async_computation.9 | async-start | bytes 33546240 | tf_op jit(solution)/shard_map/reduce_scatter | solution.py:271
  679.9 320.6 %copy-start.5 = (bf16[896,896]{1,0:T(8,128)(2,1)S(1)}, bf16[896,896]{1,0:T(8,128)(2,1)}, u32[]{:S(2)}) copy-start(bf16[896,896]{1,0:T(8,128)(2,1)} %copy.68) | copy-start | bytes 4816900
  1001.8 21.6 %slice-start = ((s8[4980736]{0:T(1024)(128)(4,1)}), s8[4194304]{0:T(1024)(128)(4,1)S(1)}, s32[]{:S(2)}) async-start(s8[4980736]{0:T(1024)(128)(4,1)} %bitcast.432), calls=%async_computation.11 | async-start | bytes 8388608
  1012.6 10.8 copy-start.13
  1012.6 10.8 slice-start.1
  1031.0 471.1 %copy-start.4 = (f32[512,896]{1,0:T(8,128)S(1)}, f32[512,896]{1,0:T(8,128)}, u32[]{:S(2)}) copy-start(f32[512,896]{1,0:T(8,128)} %copy-done.2) | copy-start | bytes 5505028
  1031.0 552.0 %all-reduce.6.cloned.1.call-start = ((), (), s32[]{:S(2)}) async-start(), calls=%async_computation.10 | async-start | bytes 7454720 | tf_op jit(solution)/shard_map/psum | solution.py:291
  1502.1 10.6 copy-start.22
  (12 other events, 25.5 us)
Sparse Core Ops, SparseCore 0:
  10.2 48.6 all-gather.9
  88.1 49.8 all-gather.7
  140.1 42.4 all-gather.11
  184.7 128.1 all-gather.15
  314.9 127.4 all-gather.13
  444.4 127.4 all-gather.17
  663.1 331.8 reduce-scatter.2
  1031.1 470.9 reduce-scatter.4
  1504.6 78.3 all-reduce.5
where the time goes:
time: 1610 us; the launch traced here: 1600 us
  waiting for transfers between devices  1240 us (77%)
  matrix products  174 us (11%)
  blocking collectives  111 us (7%)
  local copies, waits for them, and re-layouts  32.7 us (2%)
  other arithmetic  21.8 us (1%)
    reduce_scatter x1, waiting for transfers between devices, body(): lax.psum_scatter(jnp.concatenate([jnp.concatenate([outer_sum(h_one, grad_...  471 us
    reduce_scatter x1, waiting for transfers between devices, body(): lax.psum_scatter(grad_keyvals.astype(jnp.bfloat16), 'shard', scatter_dime...  315 us
    all_gather x1, waiting for transfers between devices, body(): lax.all_gather(up_weight, 'shard', axis=0, tiled=True)  126 us
    all_gather x1, waiting for transfers between devices, body(): lax.all_gather(down_weight, 'shard', axis=0, tiled=True)  118 us
    all_gather x1, waiting for transfers between devices, body(): lax.all_gather(gate_weight, 'shard', axis=0, tiled=True)  118 us
    all_gather x1, waiting for transfers between devices, body(): kv_whole = lax.all_gather(kv_local, 'shard', axis=0, tiled=True)  40.8 us
    psum x1, blocking collectives, body(): lax.psum((jnp.stack([gain_one_grad, gain_two_grad], axis=0), q_bias_sum,...  40.4 us
    dot_general x6, matrix products, outer_sum(): jnp.einsum('nr,nc->rc', left, right, preferred_element_type=jnp.float32)  36.9 us
  transfers between devices with their start and end apart: 9, of which 8 were waited for; matrix products, arithmetic and copies ran while one was open for 6% of the time, Pallas kernels for 0%

commit v1 on v0

v1 whole, which is shorter than its diff:
```python
import functools
import math

import jax
import jax.numpy as jnp
from jax import lax
from jax.experimental import pallas as pl
from jax.experimental.pallas import tpu as pltpu
from jax.sharding import PartitionSpec as P

D = 896
HEADS = 14
KV_HEADS = 2
HEAD = 64
FF = 4864
QW = 896
KW = 128
LANES = 128
TEAM = 4
FF_PART = 1280
FF_TILE = 256

EPS = 1e-06
ROPE_BASE = 1000000.0
F32 = jnp.float32
BF16 = jnp.bfloat16
VMEM_BYTES = 56 * 1024 * 1024


def dot_nt(left, right):
    return lax.dot_general(left, right, (((1,), (1,)), ((), ())), preferred_element_type=F32)


def dot_tn(left, right):
    return lax.dot_general(left, right, (((0,), (0,)), ((), ())), preferred_element_type=F32)


def dot_nn(left, right):
    return jnp.dot(left, right, preferred_element_type=F32)


def half_mask(parity, kind):
    lane = lax.broadcasted_iota(jnp.int32, (1, LANES), 1)
    return ((lane // HEAD) == parity).astype(kind)


def swap_halves(source):
    lane = lax.broadcasted_iota(jnp.int32, source.shape, 1)
    ahead = jnp.roll(source, -(HEAD // 2), axis=1)
    behind = jnp.roll(source, HEAD // 2, axis=1)
    return jnp.where(lane % HEAD < HEAD // 2, ahead, behind)


def attn_forward_kernel(me_ref, q_ref, k_ref, v_ref, o_ref, lse_ref):
    pair = pl.program_id(0)
    me = me_ref[0]
    rows = q_ref.shape[0]
    group = HEADS // KV_HEADS
    row = lax.broadcasted_iota(jnp.int32, (rows, rows), 0)
    col = lax.broadcasted_iota(jnp.int32, (rows, rows), 1)
    results = []
    for parity in range(2):
        kv_head = (2 * pair + parity) // group
        q_head = q_ref[...] * half_mask(parity, BF16)

        def scores(block):
            return dot_nt(q_head, k_ref[kv_head, pl.ds(block * rows, rows), :])

        def weigh(block, probs):
            return dot_nn(probs.astype(BF16), v_ref[kv_head, pl.ds(block * rows, rows), :])

        first = jnp.where(col <= row, scores(me), -1e30)
        top = jnp.max(first, axis=1, keepdims=True)
        probs = jnp.exp(first - top)
        total = jnp.sum(probs, axis=1, keepdims=True)
        acc = weigh(me, probs)

        def step(block, running):
            top, total, acc = running
            s = scores(block)
            new_top = jnp.maximum(top, jnp.max(s, axis=1, keepdims=True))
            shrink = jnp.exp(top - new_top)
            probs = jnp.exp(s - new_top)
            total = total * shrink + jnp.sum(probs, axis=1, keepdims=True)
            return new_top, total, acc * shrink + weigh(block, probs)

        top, total, acc = lax.fori_loop(0, me, step, (top, total, acc))
        results.append(acc / total)
        lse = jnp.broadcast_to(top + jnp.log(total), (rows, LANES))
        lse_ref[0, parity : parity + 1, :] = jnp.transpose(lse)[0:1, :]
    o_ref[...] = jnp.where(half_mask(0, jnp.int32) > 0, results[0], results[1]).astype(BF16)


def attn_forward(me, q, k_twice, v_twice):
    rows = q.shape[0]
    length = k_twice.shape[1]
    whole = pl.BlockSpec((KV_HEADS, length, LANES), lambda i, me: (0, 0, 0))
    blocks = length // rows
    return pl.pallas_call(
        attn_forward_kernel,
        grid_spec=pltpu.PrefetchScalarGridSpec(
            num_scalar_prefetch=1,
            grid=(HEADS // 2,),
            in_specs=[pl.BlockSpec((rows, LANES), lambda i, me: (0, i)), whole, whole],
            out_specs=[
                pl.BlockSpec((rows, LANES), lambda i, me: (0, i)),
                pl.BlockSpec((1, 2, rows), lambda i, me: (i, 0, 0)),
            ],
        ),
        out_shape=[
            jax.ShapeDtypeStruct((rows, QW), BF16),
            jax.ShapeDtypeStruct((HEADS // 2, 2, rows), F32),
        ],
        compiler_params=pltpu.CompilerParams(vmem_limit_bytes=VMEM_BYTES),
        cost_estimate=pl.CostEstimate(
            flops=16 * blocks * HEADS * rows * rows * HEAD // 2,
            bytes_accessed=8 * rows * QW,
            transcendentals=blocks * HEADS * rows * rows,
        ),
        name="attn_forward",
    )(me, q, k_twice, v_twice)


def attn_backward_kernel(
    me_ref,
    q_ref,
    k_ref,
    v_ref,
    o_ref,
    do_ref,
    lse_ref,
    cos_ref,
    sin_ref,
    dq_ref,
    dkv_ref,
    dk_acc,
    dv_acc,
):
    pair = pl.program_id(0)
    me = me_ref[0]
    rows = q_ref.shape[0]
    group = HEADS // KV_HEADS
    key = lax.broadcasted_iota(jnp.int32, (rows, rows), 0)
    query = lax.broadcasted_iota(jnp.int32, (rows, rows), 1)

    @pl.when(pair == 0)
    def _():
        dk_acc[...] = jnp.zeros_like(dk_acc)
        dv_acc[...] = jnp.zeros_like(dv_acc)

    products = do_ref[...].astype(F32) * o_ref[...].astype(F32)
    results = []
    for parity in range(2):
        kv_head = (2 * pair + parity) // group
        mask = half_mask(parity, BF16)
        q_head = q_ref[...] * mask
        do_head = do_ref[...] * mask
        picks = jnp.broadcast_to(half_mask(parity, F32), (8, LANES))
        delta = lax.dot_general(
            picks,
            products,
            (((1,), (1,)), ((), ())),
            precision=lax.Precision.HIGHEST,
            preferred_element_type=F32,
        )[0:1, :]
        lse = lse_ref[0, parity : parity + 1, :]

        def block_step(block, dq, masked):
            span = pl.ds(block * rows, rows)
            keys = k_ref[kv_head, span, :]
            probs = jnp.exp(dot_nt(keys, q_head) - lse)
            if masked:
                probs = jnp.where(key <= query, probs, 0.0)
            d_probs = dot_nt(v_ref[kv_head, span, :], do_head)
            d_scores = (probs * (d_probs - delta)).astype(BF16)
            dv_acc[kv_head, span, :] += dot_nn(probs.astype(BF16), do_head)
            dk_acc[kv_head, span, :] += dot_nn(d_scores, q_head)
            return dq + dot_tn(d_scores, keys)

        dq = block_step(me, jnp.zeros((rows, LANES), F32), True)
        dq = lax.fori_loop(0, me, lambda block, dq: block_step(block, dq, False), dq)
        results.append(dq)
    dq = jnp.where(half_mask(0, jnp.int32) > 0, results[0], results[1]) * HEAD ** (-0.5)
    dq_ref[...] = (dq * cos_ref[...] + swap_halves(dq * sin_ref[...])).astype(BF16)

    @pl.when(pair == HEADS // 2 - 1)
    def _():
        low = half_mask(0, jnp.int32) > 0

        def fold(block, carry):
            span = pl.ds(block * rows, rows)
            for place, acc in ((0, dk_acc), (1, dv_acc)):
                zero = acc[0, span, :]
                one = acc[1, span, :]
                zero = zero + pltpu.roll(zero, HEAD, 1)
                one = one + pltpu.roll(one, HEAD, 1)
                dkv_ref[span, place * LANES : (place + 1) * LANES] = jnp.where(
                    low, zero, one
                ).astype(BF16)
            return carry

        lax.fori_loop(0, dk_acc.shape[1] // rows, fold, 0)


def attn_backward(me, q, k_twice, v_twice, o, d_o, lse, cosine, sine):
    rows = q.shape[0]
    length = k_twice.shape[1]
    whole = pl.BlockSpec((KV_HEADS, length, LANES), lambda i, me: (0, 0, 0))
    pair = pl.BlockSpec((rows, LANES), lambda i, me: (0, i))
    table = pl.BlockSpec((rows, LANES), lambda i, me: (0, 0))
    blocks = length // rows
    return pl.pallas_call(
        attn_backward_kernel,
        grid_spec=pltpu.PrefetchScalarGridSpec(
            num_scalar_prefetch=1,
            grid=(HEADS // 2,),
            in_specs=[
                pair,
                whole,
                whole,
                pair,
                pair,
                pl.BlockSpec((1, 2, rows), lambda i, me: (i, 0, 0)),
                table,
                table,
            ],
            out_specs=[pair, pl.BlockSpec((length, 2 * KW), lambda i, me: (0, 0))],
            scratch_shapes=[
                pltpu.VMEM((KV_HEADS, length, LANES), F32),
                pltpu.VMEM((KV_HEADS, length, LANES), F32),
            ],
        ),
        out_shape=[
            jax.ShapeDtypeStruct((rows, QW), BF16),
            jax.ShapeDtypeStruct((length, 2 * KW), BF16),
        ],
        compiler_params=pltpu.CompilerParams(vmem_limit_bytes=VMEM_BYTES),
        cost_estimate=pl.CostEstimate(
            flops=40 * blocks * HEADS * rows * rows * HEAD // 2,
            bytes_accessed=16 * rows * QW,
            transcendentals=blocks * HEADS * rows * rows,
        ),
        name="attn_backward",
    )(me, q, k_twice, v_twice, o, d_o, lse, cosine, sine)


def feed_kernel(
    h_ref, c_ref, g_ref, u_ref, d_ref, out_ref, dh_ref, hid_ref, dg_ref, du_ref, out_acc, dh_acc
):
    tile = pl.program_id(0)
    h = h_ref[...]
    c = c_ref[...]
    gate = dot_nn(h, g_ref[...])
    up = dot_nn(h, u_ref[...])
    d_hid = dot_nn(c, d_ref[...])
    sig = jax.nn.sigmoid(gate)
    silu = gate * sig
    hid = (silu * up).astype(BF16)
    d_gate = (d_hid * up * sig * (1.0 + gate * (1.0 - sig))).astype(BF16)
    d_up = (d_hid * silu).astype(BF16)
    hid_ref[...] = hid
    dg_ref[...] = d_gate
    du_ref[...] = d_up
    out_part = dot_nt(hid, d_ref[...])
    dh_part = dot_nt(d_gate, g_ref[...]) + dot_nt(d_up, u_ref[...])

    @pl.when(tile == 0)
    def _():
        out_acc[...] = out_part
        dh_acc[...] = dh_part

    @pl.when(tile > 0)
    def _():
        out_acc[...] += out_part
        dh_acc[...] += dh_part

    @pl.when(tile == pl.num_programs(0) - 1)
    def _():
        out_ref[...] = out_acc[...].astype(BF16)
        dh_ref[...] = dh_acc[...].astype(BF16)


def feed(h, c, gate, up, down):
    rows = h.shape[0]
    tokens = pl.BlockSpec((rows, D), lambda i: (0, 0))
    weights = pl.BlockSpec((D, FF_TILE), lambda i: (0, i))
    hidden = pl.BlockSpec((rows, FF_TILE), lambda i: (0, i))
    return pl.pallas_call(
        feed_kernel,
        grid=(FF_PART // FF_TILE,),
        in_specs=[tokens, tokens, weights, weights, weights],
        out_specs=[tokens, tokens, hidden, hidden, hidden],
        scratch_shapes=[pltpu.VMEM((rows, D), F32), pltpu.VMEM((rows, D), F32)],
        out_shape=[jax.ShapeDtypeStruct((rows, D), BF16)] * 2
        + [jax.ShapeDtypeStruct((rows, FF_PART), BF16)] * 3,
        compiler_params=pltpu.CompilerParams(vmem_limit_bytes=VMEM_BYTES),
        cost_estimate=pl.CostEstimate(
            flops=12 * rows * D * FF_PART,
            bytes_accessed=6 * D * FF_PART + 8 * rows * D + 6 * rows * FF_PART,
            transcendentals=rows * FF_PART,
        ),
        name="feed",
    )(h, c, gate, up, down)


def ring_order(count):
    if count == 8:
        return [0, 1, 3, 5, 7, 6, 4, 2]
    return list(range(count))


class Ring:
    def __init__(self, count):
        order = ring_order(count)
        self.count = count
        self.half = count // 2
        self.ahead = [(order[i], order[(i + 1) % count]) for i in range(count)]
        self.back = [(b, a) for a, b in self.ahead]
        place = [order.index(i) for i in range(count)]
        self.order = jnp.array(order + order + order, jnp.int32)
        self.place = jnp.array(place, jnp.int32)[lax.axis_index("shard")]

    def owner(self, offset):
        return self.order[self.place + self.count + offset]

    def send(self, array, ahead):
        return lax.ppermute(array, "shard", self.ahead if ahead else self.back)

    def gather(self, array):
        rows, cols = array.shape
        cut = (cols // (2 * LANES)) * LANES
        whole = jnp.zeros((self.count * rows, cols), array.dtype)

        def put(whole, piece, offset, column):
            return lax.dynamic_update_slice(whole, piece, (self.owner(offset) * rows, column))

        whole = put(whole, array, 0, 0)
        right = left = array
        for step in range(1, self.half):
            right = self.send(right, True)
            left = self.send(left, False)
            whole = put(whole, right, -step, 0)
            whole = put(whole, left, step, 0)
        whole = put(whole, self.send(right[:, :cut], True), self.half, 0)
        return put(whole, self.send(left[:, cut:], False), self.half, cut)

    def scatter_sum(self, array):
        rows = array.shape[0] // self.count
        cols = array.shape[1]
        cut = (cols // (2 * LANES)) * LANES

        def chunk(offset):
            return lax.dynamic_slice(array, (self.owner(offset) * rows, 0), (rows, cols))

        def add(left, right):
            return (left.astype(F32) + right.astype(F32)).astype(BF16)

        far = chunk(self.half)
        right = self.send(far[:, :cut], True)
        left = self.send(far[:, cut:], False)
        for step in range(self.half - 1, 0, -1):
            near = chunk(step)
            if step == self.half - 1:
                right = jnp.concatenate([add(near[:, :cut], right), near[:, cut:]], axis=1)
            else:
                right = add(near, right)
            right = self.send(right, True)
            near = chunk(-step)
            if step == self.half - 1:
                left = jnp.concatenate([near[:, :cut], add(near[:, cut:], left)], axis=1)
            else:
                left = add(near, left)
            left = self.send(left, False)
        return chunk(0).astype(F32) + right.astype(F32) + left.astype(F32)


def team_send(array, bit):
    return lax.ppermute(array, "rep", [(i, i ^ bit) for i in range(lax.axis_size("rep"))])


def team_sum(mine, core, cross, both):
    gathered = (cross.astype(F32) + team_send(both, 1).astype(F32)).astype(BF16)
    return (
        mine.astype(F32)
        + team_send(core, 1).astype(F32)
        + team_send(gathered, 2).astype(F32)
    )


def rope_tables(positions):
    half_width = HEAD // 2
    inverse = jnp.exp(
        jnp.arange(half_width, dtype=F32) * (-2.0 * math.log(ROPE_BASE) / HEAD)
    )
    angles = positions.astype(F32)[:, None] * inverse[None, :]
    cosine = jnp.cos(angles)
    sine = jnp.sin(angles)
    return (
        jnp.concatenate([cosine] * 4, axis=1),
        jnp.concatenate([-sine, sine, -sine, sine], axis=1),
    )


def rotate(source, cosine, sine):
    times = source.shape[1] // LANES
    return source * jnp.tile(cosine, (1, times)) + swap_halves(source) * jnp.tile(sine, (1, times))


def rotate_back(source, cosine, sine):
    times = source.shape[1] // LANES
    return source * jnp.tile(cosine, (1, times)) + swap_halves(source * jnp.tile(sine, (1, times)))


def norm_back(grad_normed, normed, inv_scale, gain_row):
    scaled = grad_normed * gain_row
    return inv_scale * (scaled - normed * jnp.mean(scaled * normed, axis=1, keepdims=True))


def body(
    hidden_in,
    cotangent,
    norm_gains,
    q_bias,
    kv_bias,
    q_weight,
    kv_weight,
    out_weight,
    gate_weight,
    up_weight,
    down_weight,
):
    tok_rows = hidden_in.shape[1]
    shard_count = lax.axis_size("shard")
    rep_count = lax.axis_size("rep")
    shard_place = lax.axis_index("shard")
    rep_place = lax.axis_index("rep")
    team_place = rep_place % TEAM
    row_share = D // shard_count
    kv_share = 2 * KW // shard_count
    ring = Ring(shard_count)

    small = jnp.concatenate([norm_gains[0], norm_gains[1], q_bias, kv_bias])
    spare = jnp.pad(small[None, :], ((0, 15), (0, QW + 2 * KW - small.shape[0])))
    qkv_piece = jnp.concatenate(
        [jnp.concatenate([q_weight, kv_weight], axis=1), spare], axis=0
    )
    qkv_rows = row_share + 16
    qkv_all = ring.gather(qkv_piece).reshape(shard_count, qkv_rows, QW + 2 * KW)
    qkv_full = qkv_all[:, :row_share].reshape(D, QW + 2 * KW)
    smalls = qkv_all[:, row_share].astype(F32)
    gain_one = smalls[:, :row_share].reshape(D)
    gain_two = smalls[:, row_share : 2 * row_share].reshape(D)
    q_bias_all = smalls[:, 2 * row_share : 3 * row_share].reshape(QW)
    kv_bias_all = smalls[:, 3 * row_share : 3 * row_share + kv_share].reshape(2 * KW)
    q_full = qkv_full[:, :QW]
    kv_full = qkv_full[:, QW:]

    grad_out = cotangent[0]
    inputs = hidden_in[0].astype(F32)
    inv_one = lax.rsqrt(jnp.mean(inputs * inputs, axis=1, keepdims=True) + EPS)
    normed_one = inputs * inv_one
    h_one = (normed_one * gain_one).astype(BF16)
    positions = shard_place * tok_rows + jnp.arange(tok_rows, dtype=jnp.int32)
    cosine, sine = rope_tables(positions)
    keyvals = dot_nn(h_one, kv_full) + kv_bias_all
    kv_local = jnp.concatenate(
        [rotate(keyvals[:, :KW], cosine, sine), keyvals[:, KW:]], axis=1
    ).astype(BF16)
    kv_whole = ring.gather(kv_local)
    queries = dot_nn(h_one, q_full) + q_bias_all
    q_scaled = rotate(queries, cosine, sine).astype(BF16) * jnp.asarray(HEAD ** (-0.5), BF16)
    out_full = ring.gather(out_weight)

    def quarter(weight):
        padded = jnp.pad(weight, ((0, 0), (0, TEAM * FF_PART - FF)))
        return lax.dynamic_slice_in_dim(padded, team_place * FF_PART, FF_PART, 1)

    gate_full = ring.gather(quarter(gate_weight))
    up_full = ring.gather(quarter(up_weight))
    down_full = ring.gather(quarter(down_weight))

    me = shard_place.astype(jnp.int32).reshape(1)
    heads = [kv_whole[:, HEAD * i : HEAD * (i + 1)] for i in range(2 * KV_HEADS)]
    k_twice = jnp.stack([jnp.concatenate([h, h], axis=1) for h in heads[:KV_HEADS]])
    v_twice = jnp.stack([jnp.concatenate([h, h], axis=1) for h in heads[KV_HEADS:]])
    attn_b, lse = attn_forward(me, q_scaled, k_twice, v_twice)

    middle = inputs + dot_nt(attn_b, out_full)
    inv_two = lax.rsqrt(jnp.mean(middle * middle, axis=1, keepdims=True) + EPS)
    normed_two = middle * inv_two
    h_two = (normed_two * gain_two).astype(BF16)

    c_core = team_send(grad_out, 1)
    c_cross = team_send(grad_out, 2)
    c_both = team_send(c_cross, 1)
    h_core = team_send(h_two, 1)
    h_cross = team_send(h_two, 2)
    h_both = team_send(h_cross, 1)
    sets = ((h_two, grad_out), (h_core, c_core), (h_cross, c_cross), (h_both, c_both))
    done = [feed(h, c, gate_full, up_full, down_full) for h, c in sets]
    grad_h_two = team_sum(*[one[1] for one in done])
    out_sum = team_sum(*[one[0] for one in done])
    output = middle + out_sum

    h_sets = jnp.concatenate([h for h, _ in sets], axis=0)
    c_sets = jnp.concatenate([c for _, c in sets], axis=0)
    hid_sets, dg_sets, du_sets = (
        jnp.concatenate([one[i] for one in done], axis=0) for i in (2, 3, 4)
    )
    feed_grads = [
        dot_tn(left, right).astype(BF16)
        for left, right in ((h_sets, dg_sets), (h_sets, du_sets), (c_sets, hid_sets))
    ]

    gain_two_grad = jnp.sum(grad_h_two * normed_two, axis=0)
    grad_middle = grad_out.astype(F32) + norm_back(grad_h_two, normed_two, inv_two, gain_two)
    grad_branch_b = grad_middle.astype(BF16)
    out_grad = dot_tn(grad_branch_b, attn_b)
    grad_attn = dot_nn(grad_branch_b, out_full).astype(BF16)
    grad_q_b, grad_kv_parts = attn_backward(
        me, q_scaled, k_twice, v_twice, attn_b, grad_attn, lse, cosine, sine
    )
    grad_kv_mine = ring.scatter_sum(grad_kv_parts)
    grad_kv_b = jnp.concatenate(
        [rotate_back(grad_kv_mine[:, :KW], cosine, sine), grad_kv_mine[:, KW:]], axis=1
    ).astype(BF16)
    q_bias_sum = jnp.sum(grad_q_b.astype(F32), axis=0)
    kv_bias_sum = jnp.sum(grad_kv_b.astype(F32), axis=0)
    grad_h_one = dot_nt(grad_q_b, q_full) + dot_nt(grad_kv_b, kv_full)
    gain_one_grad = jnp.sum(grad_h_one * normed_one, axis=0)
    input_grad = (grad_middle + norm_back(grad_h_one, normed_one, inv_one, gain_one)).astype(BF16)

    feed_rows = [ring.scatter_sum(grad).astype(BF16) for grad in feed_grads]
    teams = rep_count // TEAM
    if teams > 1:
        across = [[t * TEAM + i for t in range(teams)] for i in range(TEAM)]
        feed_rows = [lax.psum(rows, "rep", axis_index_groups=across) for rows in feed_rows]

    def team_columns(rows):
        core = team_send(rows, 1)
        cross = team_send(rows, 2)
        both = team_send(cross, 1)
        whole = jnp.zeros((row_share, TEAM * FF_PART), BF16)
        for bit, part in ((0, rows), (1, core), (2, cross), (3, both)):
            whole = lax.dynamic_update_slice(whole, part, (0, (team_place ^ bit) * FF_PART))
        return whole[:, :FF].astype(F32)

    gate_grad, up_grad, down_grad = (team_columns(rows) for rows in feed_rows)

    attn_grads = jnp.concatenate(
        [dot_tn(h_one, grad_q_b), dot_tn(h_one, grad_kv_b), out_grad], axis=1
    ).astype(BF16)
    attn_rows = ring.scatter_sum(attn_grads).astype(BF16)
    attn_rows = (attn_rows.astype(F32) + team_send(attn_rows, 1).astype(F32)).astype(BF16)
    attn_rows = attn_rows.astype(F32) + team_send(attn_rows, 2).astype(F32)
    if teams > 1:
        attn_rows = lax.psum(attn_rows.astype(BF16), "rep", axis_index_groups=across).astype(F32)

    gains_full, q_bias_full, kv_bias_full = lax.psum(
        (jnp.stack([gain_one_grad, gain_two_grad], axis=0), q_bias_sum, kv_bias_sum),
        ("rep", "shard"),
    )
    gains_grad = lax.dynamic_slice_in_dim(gains_full, shard_place * row_share, row_share, 1)
    q_bias_grad = lax.dynamic_slice_in_dim(q_bias_full, shard_place * row_share, row_share, 0)
    kv_bias_grad = lax.dynamic_slice_in_dim(kv_bias_full, shard_place * kv_share, kv_share, 0)
    return (
        output.astype(BF16)[None],
        input_grad[None],
        gains_grad,
        q_bias_grad,
        kv_bias_grad,
        attn_rows[:, :QW],
        attn_rows[:, QW : QW + 2 * KW],
        attn_rows[:, QW + 2 * KW :],
        gate_grad,
        up_grad,
        down_grad,
    )


def solution(mesh):
    tokens = P("rep", "shard", None)
    rows = P("shard", None)
    placed = (tokens, tokens, P(None, "shard"), P("shard"), P("shard")) + (rows,) * 6
    return jax.shard_map(body, mesh=mesh, in_specs=placed, out_specs=placed, check_vma=False)
```

time: 1610 us -> 811 us (0.50)
  waiting for transfers between devices: 1240 us -> 213 us
  starting transfers between devices: 0.53 us -> 240 us
  matrix products: 174 us -> 40.9 us
  Pallas kernels: 0 us -> 100 us
  blocking collectives: 111 us -> 42 us
  local copies, waits for them, and re-layouts: 32.7 us -> 90 us
  other arithmetic: 21.8 us -> 47.5 us
    reduce_scatter x2 -> x0, waiting for transfers between devices: 786 us -> none  [the longest x1 471 us: body(): lax.psum_scatter(jnp.concatenate([jnp.concatenate([outer_sum(h_one, grad_...]
    all_gather x6 -> x0, waiting for transfers between devices: 430 us -> none  [the longest x1 126 us: body(): lax.all_gather(up_weight, 'shard', axis=0, tiled=True)]
    ppermute x0 -> x111, starting transfers between devices: none -> 240 us  [the longest x88 228 us: send(): return lax.ppermute(array, 'shard', self.ahead if ahead else self.back)]
    ppermute x0 -> x111, waiting for transfers between devices: none -> 213 us  [the longest x88 189 us: send(): return lax.ppermute(array, 'shard', self.ahead if ahead else self.back)]
    dot_general x36 -> x12, matrix products: 174 us -> 40.9 us  [the longest x6 26.9 us: dot_tn(): lax.dot_general(left, right, (((0,), (0,)), ((), ())), preferred_element_...]
    pallas_call x0 -> x6, Pallas kernels: none -> 100 us  [the longest x4 60.4 us: feed(): pl.pallas_call(feed_kernel, grid=(FF_PART // FF_TILE,), in_specs=[tokens,...]
    all_gather x2 -> x0, blocking collectives: 47.7 us -> none  [the longest x1 31.3 us: body(): lax.all_gather(kv_weight, 'shard', axis=0, tiled=True)]
    dynamic_update_slice x0 -> x61, local copies, waits for them, and re-layouts: none -> 45.9 us  [the longest x52 39.6 us: put(): lax.dynamic_update_slice(whole, piece, (self.owner(offset) * rows, column))]
  transfers between devices with their start and end apart: 9 -> 111, of which waited for: 8 -> 59; matrix products, arithmetic and copies ran while one was open for 6% -> 21% of each run, Pallas kernels for 0% -> 13%
where the time goes in v1:
time: 811 us; the launch traced here: 802 us
  starting transfers between devices  240 us (30%)
  waiting for transfers between devices  213 us (26%)
  Pallas kernels  100 us (12%)
  local copies, waits for them, and re-layouts  90 us (11%)
  other arithmetic  47.5 us (6%)
  blocking collectives  42 us (5%)
  matrix products  40.9 us (5%)
  between operations  28.3 us (3%)
    ppermute x88, starting transfers between devices, send(): return lax.ppermute(array, 'shard', self.ahead if ahead else self.back)  228 us
    ppermute x88, waiting for transfers between devices, send(): return lax.ppermute(array, 'shard', self.ahead if ahead else self.back)  189 us
    pallas_call x4, Pallas kernels, feed(): pl.pallas_call(feed_kernel, grid=(FF_PART // FF_TILE,), in_specs=[tokens,...  60.4 us
    psum x1, blocking collectives, body(): lax.psum((jnp.stack([gain_one_grad, gain_two_grad], axis=0), q_bias_sum,...  42 us
    dynamic_update_slice x52, local copies, waits for them, and re-layouts, put(): lax.dynamic_update_slice(whole, piece, (self.owner(offset) * rows, column))  39.6 us
    dot_general x6, matrix products, dot_tn(): lax.dot_general(left, right, (((0,), (0,)), ((), ())), preferred_element_...  26.9 us
    ppermute x23, waiting for transfers between devices, team_send(): lax.ppermute(array, 'rep', [(i, i ^ bit) for i in range(lax.axis_size('re...  25 us
    pallas_call x1, Pallas kernels, attn_backward(): pl.pallas_call(attn_backward_kernel, grid_spec=pltpu.PrefetchScalarGridSp...  24.2 us
  transfers between devices with their start and end apart: 111, of which 59 were waited for; matrix products, arithmetic and copies ran while one was open for 21% of the time, Pallas kernels for 13%

profile of v1, /device:TPU:0, one launch (start us, length us, event | category | flops | bytes accessed | tf_op | source)
XLA Modules:
  0.0 802.2 jit_solution(10915100467255312772)
XLA Ops:
  217.5 15.9 %attn_forward.1 = (bf16[512,896]{1,0:T(8,128)(2,1)}, f32[7,2,512]{2,1,0:T(2,128)}) custom-call(s32[1]{0:T(128)} %bitcast.1.me_ref, bf16[512,896]{1,0:T(8,128)(2,1)} %fusion.62.q_ref, bf16[2,4096,128]{2,1,0:T(8,128)(2,1)} %pad_maximum_fusion.2.k_ref, bf16[2,4096,128]{2,1,0:T(8,128)(2,1)} %pad_maximum_fusion.3.v_ref), custom_call_target="tpu_custom_call" | custom-call | flops 15032385536 | bytes 3670016 | tf_op jit(solution)/shard_map/attn_forward/pallas_call | solution.py:99
  241.3 15.1 %feed.4 = (bf16[512,896]{1,0:T(8,128)(2,1)}, bf16[512,896]{1,0:T(8,128)(2,1)}, bf16[512,1280]{1,0:T(8,128)(2,1)}, bf16[512,1280]{1,0:T(8,128)(2,1)}, bf16[512,1280]{1,0:T(8,128)(2,1)}) custom-call(bf16[512,896]{1,0:T(8,128)(2,1)} %copy-done.16, bf16[512,896]{1,0:T(8,128)(2,1)} %bitcast.53.c_ref, ...), custom_call_target="tpu_custom_call" | custom-call | flops 7046430720 | bytes 14483456 | tf_op jit(solution)/shard_map/feed/pallas_call | solution.py:288
  257.5 15.1 %feed.5 = (bf16[512,896]{1,0:T(8,128)(2,1)}, bf16[512,896]{1,0:T(8,128)(2,1)}, bf16[512,1280]{1,0:T(8,128)(2,1)}, bf16[512,1280]{1,0:T(8,128)(2,1)}, bf16[512,1280]{1,0:T(8,128)(2,1)}) custom-call(bf16[512,896]{1,0:T(8,128)(2,1)} %copy-done.37, bf16[512,896]{1,0:T(8,128)(2,1)} %collective-permute-done.49.c_ref, ...), custom_call_target="tpu_custom_call" | custom-call | flops 7046430720 | bytes 14483456 | tf_op jit(solution)/shard_map/feed/pallas_call | solution.py:288
  273.0 15.1 %feed.6 = (bf16[512,896]{1,0:T(8,128)(2,1)}, bf16[512,896]{1,0:T(8,128)(2,1)}, bf16[512,1280]{1,0:T(8,128)(2,1)}, bf16[512,1280]{1,0:T(8,128)(2,1)}, bf16[512,1280]{1,0:T(8,128)(2,1)}) custom-call(bf16[512,896]{1,0:T(8,128)(2,1)} %collective-permute-done.51.h_ref, bf16[512,896]{1,0:T(8,128)(2,1)} %collective-permute-done.52.c_ref, ...), custom_call_target="tpu_custom_call" | custom-call | flops 7046430720 | bytes 14483456 | tf_op jit(solution)/shard_map/feed/pallas_call | solution.py:288
  290.0 15.2 %feed.7 = (bf16[512,896]{1,0:T(8,128)(2,1)}, bf16[512,896]{1,0:T(8,128)(2,1)}, bf16[512,1280]{1,0:T(8,128)(2,1)}, bf16[512,1280]{1,0:T(8,128)(2,1)}, bf16[512,1280]{1,0:T(8,128)(2,1)}) custom-call(bf16[512,896]{1,0:T(8,128)(2,1)} %copy-done.41, bf16[512,896]{1,0:T(8,128)(2,1)} %copy-done.39, bf16[896,1280]{1,0:T(8,128)(2,1)} %constant_dynamic-update-slice_fusion.62.g_ref, ...), custom_call_target="tpu_custom_call" | custom-call | flops 7046430720 | bytes 14483456 | tf_op jit(solution)/shard_map/feed/pallas_call | solution.py:288
  314.0 11.4 %collective-permute-start.78 = (bf16[112,640]{1,0:T(8,128)(2,1)S(1)}, bf16[112,640]{1,0:T(8,128)(2,1)S(1)}, u32[]{:S(2)}, u32[]{:S(2)}) collective-permute-start(bf16[112,640]{1,0:T(8,128)(2,1)S(1)} %get-tuple-element.141), channel_id=1, source_target_pairs={{0,1},{1,3},{3,5},{5,7},{7,6},{6,4},{4,2},{2,0},{8,9},{9,11},{11,1... | collective-permute-start | bytes 430088 | tf_op jit(solution)/shard_map/ppermute | solution.py:327
  325.3 9.7 %collective-permute-start.82 = (bf16[112,640]{1,0:T(8,128)(2,1)S(1)}, bf16[112,640]{1,0:T(8,128)(2,1)S(1)}, u32[]{:S(2)}, u32[]{:S(2)}) collective-permute-start(bf16[112,640]{1,0:T(8,128)(2,1)S(1)} %get-tuple-element.143), channel_id=1, source_target_pairs={{1,0},{3,1},{5,3},{7,5},{6,7},{4,6},{2,4},{0,2},{9,8},{11,9},{13,1... | collective-permute-start | bytes 430088 | tf_op jit(solution)/shard_map/ppermute | solution.py:327
  342.6 8.3 %fusion.31 = bf16[896,1280]{1,0:T(8,128)(2,1)S(1)} fusion(bf16[512,1280]{1,0:T(8,128)(2,1)} %get-tuple-element.58, bf16[512,1280]{1,0:T(8,128)(2,1)} %get-tuple-element.57, bf16[512,1280]{1,0:T(8,128)(2,1)} %get-tuple-element.56, bf16[512,1280]{1,0:T(8,128)(2,1)} %get-tuple-element.55, bf16[512,896]{1,0:T(8,128)(2,1)S(1)} %copy-done.40, ...), kind=kOutput, calls=%fused_computation.33 | convolution fusion | flops 4734418944 | bytes 11206656 | tf_op jit(solution)/shard_map/dot_general | solution.py:35
  351.0 10.4 %collective-permute-start.89 = (bf16[112,640]{1,0:T(8,128)(2,1)S(1)}, bf16[112,640]{1,0:T(8,128)(2,1)S(1)}, u32[]{:S(2)}, u32[]{:S(2)}) collective-permute-start(bf16[112,640]{1,0:T(8,128)(2,1)S(1)} %get-tuple-element.133), channel_id=1, source_target_pairs={{0,1},{1,3},{3,5},{5,7},{7,6},{6,4},{4,2},{2,0},{8,9},{9,11},{11,1... | collective-permute-start | bytes 430088 | tf_op jit(solution)/shard_map/ppermute | solution.py:327
  361.4 8.8 %collective-permute-start.93 = (bf16[112,640]{1,0:T(8,128)(2,1)S(1)}, bf16[112,640]{1,0:T(8,128)(2,1)S(1)}, u32[]{:S(2)}, u32[]{:S(2)}) collective-permute-start(bf16[112,640]{1,0:T(8,128)(2,1)S(1)} %get-tuple-element.135), channel_id=1, source_target_pairs={{1,0},{3,1},{5,3},{7,5},{6,7},{4,6},{2,4},{0,2},{9,8},{11,9},{13,1... | collective-permute-start | bytes 430088 | tf_op jit(solution)/shard_map/ppermute | solution.py:327
  373.9 10.1 %collective-permute-start.100 = (bf16[112,640]{1,0:T(8,128)(2,1)S(1)}, bf16[112,640]{1,0:T(8,128)(2,1)S(1)}, u32[]{:S(2)}, u32[]{:S(2)}) collective-permute-start(bf16[112,640]{1,0:T(8,128)(2,1)S(1)} %get-tuple-element.125), channel_id=1, source_target_pairs={{0,1},{1,3},{3,5},{5,7},{7,6},{6,4},{4,2},{2,0},{8,9},{9,11},{11,1... | collective-permute-start | bytes 430088 | tf_op jit(solution)/shard_map/ppermute | solution.py:327
  384.5 9.4 %collective-permute-start.104 = (bf16[112,640]{1,0:T(8,128)(2,1)S(1)}, bf16[112,640]{1,0:T(8,128)(2,1)S(1)}, u32[]{:S(2)}, u32[]{:S(2)}) collective-permute-start(bf16[112,640]{1,0:T(8,128)(2,1)S(1)} %get-tuple-element.127), channel_id=1, source_target_pairs={{1,0},{3,1},{5,3},{7,5},{6,7},{4,6},{2,4},{0,2},{9,8},{11,9},{13,1... | collective-permute-start | bytes 430088 | tf_op jit(solution)/shard_map/ppermute | solution.py:327
  397.1 9.8 %collective-permute-start.79 = (bf16[112,1280]{1,0:T(8,128)(2,1)S(1)}, bf16[112,1280]{1,0:T(8,128)(2,1)S(1)}, u32[]{:S(2)}, u32[]{:S(2)}) collective-permute-start(bf16[112,1280]{1,0:T(8,128)(2,1)S(1)} %pad_maximum_fusion.8), channel_id=1, source_target_pairs={{0,1},{1,3},{3,5},{5,7},{7,6},{6,4},{4,2},{2,0},{8,9},{9,11},{11,1... | collective-permute-start | bytes 860168 | tf_op jit(solution)/shard_map/ppermute | solution.py:327
  507.0 17.0 %collective-permute-done.56 = bf16[512,896]{1,0:T(8,128)(2,1)S(1)} collective-permute-done((bf16[512,896]{1,0:T(8,128)(2,1)S(1)}, bf16[512,896]{1,0:T(8,128)(2,1)S(1)}, u32[]{:S(2)}, u32[]{:S(2)}) %collective-permute-start.56) | collective-permute-done | bytes 917536 | tf_op jit(solution)/shard_map/ppermute | solution.py:378
  531.2 24.2 %attn_backward.1 = (bf16[512,896]{1,0:T(8,128)(2,1)}, bf16[4096,256]{1,0:T(8,128)(2,1)}) custom-call(s32[1]{0:T(128)} %bitcast.1.me_ref, bf16[512,896]{1,0:T(8,128)(2,1)} %fusion.62.q_ref, bf16[2,4096,128]{2,1,0:T(8,128)(2,1)} %pad_maximum_fusion.2.k_ref, bf16[2,4096,128]{2,1,0:T(8,128)(2,1)} %pad_maximum_fusion.3.v_ref, ...), custom_call_target="tpu_custom_call" | custom-call | flops 37580963840 | bytes 7340032 | tf_op jit(solution)/shard_map/attn_backward/pallas_call | solution.py:212
  556.7 14.1 %collective-permute-start.60 = (bf16[512,128]{1,0:T(8,128)(2,1)S(1)}, bf16[512,128]{1,0:T(8,128)(2,1)S(1)}, u32[]{:S(2)}, u32[]{:S(2)}) collective-permute-start(bf16[512,128]{1,0:T(8,128)(2,1)S(1)} %get-tuple-element.149), channel_id=1, source_target_pairs={{0,1},{1,3},{3,5},{5,7},{7,6},{6,4},{4,2},{2,0},{8,9},{9,11},{11,1... | collective-permute-start | bytes 393224 | tf_op jit(solution)/shard_map/ppermute | solution.py:327
  570.8 10.5 %collective-permute-start.64 = (bf16[512,128]{1,0:T(8,128)(2,1)S(1)}, bf16[512,128]{1,0:T(8,128)(2,1)S(1)}, u32[]{:S(2)}, u32[]{:S(2)}) collective-permute-start(bf16[512,128]{1,0:T(8,128)(2,1)S(1)} %get-tuple-element.151), channel_id=1, source_target_pairs={{1,0},{3,1},{5,3},{7,5},{6,7},{4,6},{2,4},{0,2},{9,8},{11,9},{13,1... | collective-permute-start | bytes 393224 | tf_op jit(solution)/shard_map/ppermute | solution.py:327
  584.2 13.9 %collective-permute-done.64 = bf16[512,128]{1,0:T(8,128)(2,1)S(1)} collective-permute-done((bf16[512,128]{1,0:T(8,128)(2,1)S(1)}, bf16[512,128]{1,0:T(8,128)(2,1)S(1)}, u32[]{:S(2)}, u32[]{:S(2)}) %collective-permute-start.64) | collective-permute-done | bytes 131104 | tf_op jit(solution)/shard_map/ppermute | solution.py:327
  599.1 24.8 %collective-permute-start.61 = (bf16[512,256]{1,0:T(8,128)(2,1)S(1)}, bf16[512,256]{1,0:T(8,128)(2,1)S(1)}, u32[]{:S(2)}, u32[]{:S(2)}) collective-permute-start(bf16[512,256]{1,0:T(8,128)(2,1)S(1)} %pad_maximum_fusion.17), channel_id=1, source_target_pairs={{0,1},{1,3},{3,5},{5,7},{7,6},{6,4},{4,2},{2,0},{8,9},{9,11},{11,1... | collective-permute-start | bytes 786440 | tf_op jit(solution)/shard_map/ppermute | solution.py:327
  627.8 15.8 %collective-permute-start.65 = (bf16[512,256]{1,0:T(8,128)(2,1)S(1)}, bf16[512,256]{1,0:T(8,128)(2,1)S(1)}, u32[]{:S(2)}, u32[]{:S(2)}) collective-permute-start(bf16[512,256]{1,0:T(8,128)(2,1)S(1)} %pad_maximum_fusion.18), channel_id=1, source_target_pairs={{1,0},{3,1},{5,3},{7,5},{6,7},{4,6},{2,4},{0,2},{9,8},{11,9},{13,1... | collective-permute-start | bytes 786440 | tf_op jit(solution)/shard_map/ppermute | solution.py:327
  643.7 10.1 %collective-permute-start.62 = (bf16[512,256]{1,0:T(8,128)(2,1)S(1)}, bf16[512,256]{1,0:T(8,128)(2,1)S(1)}, u32[]{:S(2)}, u32[]{:S(2)}) collective-permute-start(bf16[512,256]{1,0:T(8,128)(2,1)S(1)} %add_convert_fusion.29), channel_id=1, source_target_pairs={{0,1},{1,3},{3,5},{5,7},{7,6},{6,4},{4,2},{2,0},{8,9},{9,11},{11,1... | collective-permute-start | bytes 786440 | tf_op jit(solution)/shard_map/ppermute | solution.py:327
  695.9 9.5 %collective-permute-done.69 = bf16[112,2048]{0,1:T(8,128)(2,1)S(1)} collective-permute-done((bf16[112,2048]{0,1:T(8,128)(2,1)S(1)}, bf16[112,2048]{0,1:T(8,128)(2,1)S(1)}, u32[]{:S(2)}, u32[]{:S(2)}) %collective-permute-start.69) | collective-permute-done | bytes 458784 | tf_op jit(solution)/shard_map/ppermute | solution.py:327
  720.9 8.4 %collective-permute-done.74 = bf16[112,2048]{0,1:T(8,128)(2,1)S(1)} collective-permute-done((bf16[112,2048]{0,1:T(8,128)(2,1)S(1)}, bf16[112,2048]{0,1:T(8,128)(2,1)S(1)}, u32[]{:S(2)}, u32[]{:S(2)}) %collective-permute-start.74) | collective-permute-done | bytes 458784 | tf_op jit(solution)/shard_map/ppermute | solution.py:327
  741.7 42.0 %all-reduce.4 = (f32[2,896]{1,0:T(2,128)S(1)}, f32[896]{0:T(1024)S(1)}, f32[256]{0:T(256)S(1)}) all-reduce(f32[2,896]{1,0:T(2,128)S(1)} %pad_maximum_fusion.22, f32[896]{0:T(1024)S(1)} %convert_reduce_fusion, f32[256]{0:T(256)S(1)} %convert_reduce_fusion.1), channel_id=1, replica_groups=mesh['rep'=4,'shard'=8] {'rep','shard'}, use_global_device_ids=true, to_apply=%region_6.7 | all-reduce | flops 2944 | bytes 23552 | tf_op jit(solution)/shard_map/psum | solution.py:559
  (508 shorter events, 429.4 us)
Async XLA Ops:
  17.0 67.1 %collective-permute-start = (bf16[128,1152]{1,0:T(8,128)(2,1)}, bf16[128,1152]{1,0:T(8,128)(2,1)}, u32[]{:S(2)}, u32[]{:S(2)}) collective-permute-start(bf16[128,1152]{1,0:T(8,128)(2,1)} %get-tuple-element.175), channel_id=1, source_target_pairs={{0,1},{1,3},{3,5},{5,7},{7,6},{6,4},{4,2},{2,0},{8,9},{9,11},{11,1... | collective-permute-start | bytes 884744 | tf_op jit(solution)/shard_map/ppermute | solution.py:327
  20.0 65.6 %collective-permute-start.1 = (bf16[128,1152]{1,0:T(8,128)(2,1)}, bf16[128,1152]{1,0:T(8,128)(2,1)}, u32[]{:S(2)}, u32[]{:S(2)}) collective-permute-start(bf16[128,1152]{1,0:T(8,128)(2,1)} %get-tuple-element.175), channel_id=1, source_target_pairs={{1,0},{3,1},{5,3},{7,5},{6,7},{4,6},{2,4},{0,2},{9,8},{11,9},{13,1... | collective-permute-start | bytes 884744 | tf_op jit(solution)/shard_map/ppermute | solution.py:327
  20.0 42.1 %collective-permute-start.16 = (bf16[112,896]{1,0:T(8,128)(2,1)}, bf16[112,896]{1,0:T(8,128)(2,1)}, u32[]{:S(2)}, u32[]{:S(2)}) collective-permute-start(bf16[112,896]{1,0:T(8,128)(2,1)} %param.20), channel_id=1, source_target_pairs={{0,1},{1,3},{3,5},{5,7},{7,6},{6,4},{4,2},{2,0},{8,9},{9,11},{11,1... | collective-permute-start | bytes 602120 | tf_op jit(solution)/shard_map/ppermute | solution.py:327
  22.0 41.9 %collective-permute-start.17 = (bf16[112,896]{1,0:T(8,128)(2,1)}, bf16[112,896]{1,0:T(8,128)(2,1)}, u32[]{:S(2)}, u32[]{:S(2)}) collective-permute-start(bf16[112,896]{1,0:T(8,128)(2,1)} %param.20), channel_id=1, source_target_pairs={{1,0},{3,1},{5,3},{7,5},{6,7},{4,6},{2,4},{0,2},{9,8},{11,9},{13,1... | collective-permute-start | bytes 602120 | tf_op jit(solution)/shard_map/ppermute | solution.py:327
  25.2 42.3 %collective-permute-start.24 = (bf16[112,1280]{1,0:T(8,128)(2,1)}, bf16[112,1280]{1,0:T(8,128)(2,1)}, u32[]{:S(2)}, u32[]{:S(2)}) collective-permute-start(bf16[112,1280]{1,0:T(8,128)(2,1)} %get-tuple-element.110), channel_id=1, source_target_pairs={{0,1},{1,3},{3,5},{5,7},{7,6},{6,4},{4,2},{2,0},{8,9},{9,11},{11,1... | collective-permute-start | bytes 860168 | tf_op jit(solution)/shard_map/ppermute | solution.py:327
  77.4 159.3 %collective-permute-start.52 = (bf16[512,896]{1,0:T(8,128)(2,1)}, bf16[512,896]{1,0:T(8,128)(2,1)}, u32[]{:S(2)}, u32[]{:S(2)}) collective-permute-start(bf16[512,896]{1,0:T(8,128)(2,1)} %bitcast.53.c_ref), channel_id=1, source_target_pairs={{0,16},{8,24},{16,0},{24,8},{1,17},{9,25},{17,1},{25,9},{2,18},{10... | collective-permute-start | bytes 2752520 | tf_op jit(solution)/shard_map/ppermute | solution.py:378
  79.6 176.9 %collective-permute-start.49 = (bf16[512,896]{1,0:T(8,128)(2,1)}, bf16[512,896]{1,0:T(8,128)(2,1)}, u32[]{:S(2)}, u32[]{:S(2)}) collective-permute-start(bf16[512,896]{1,0:T(8,128)(2,1)} %bitcast.53.c_ref), channel_id=1, source_target_pairs={{0,8},{8,0},{16,24},{24,16},{1,9},{9,1},{17,25},{25,17},{2,10},{10... | collective-permute-start | bytes 2752520 | tf_op jit(solution)/shard_map/ppermute | solution.py:378
  154.3 83.6 %collective-permute-start.39 = (bf16[112,640]{1,0:T(8,128)(2,1)}, bf16[112,640]{1,0:T(8,128)(2,1)}, u32[]{:S(2)}, u32[]{:S(2)}) collective-permute-start(bf16[112,640]{1,0:T(8,128)(2,1)} %slice.357), channel_id=1, source_target_pairs={{1,0},{3,1},{5,3},{7,5},{6,7},{4,6},{2,4},{0,2},{9,8},{11,9},{13,1... | collective-permute-start | bytes 430088 | tf_op jit(solution)/shard_map/ppermute | solution.py:327
  205.8 33.7 %collective-permute-start.46 = (bf16[112,640]{1,0:T(8,128)(2,1)S(1)}, bf16[112,640]{1,0:T(8,128)(2,1)S(1)}, u32[]{:S(2)}, u32[]{:S(2)}) collective-permute-start(bf16[112,640]{1,0:T(8,128)(2,1)S(1)} %copy-done.22), channel_id=1, source_target_pairs={{0,1},{1,3},{3,5},{5,7},{7,6},{6,4},{4,2},{2,0},{8,9},{9,11},{11,1... | collective-permute-start | bytes 430088 | tf_op jit(solution)/shard_map/ppermute | solution.py:327
  239.5 48.7 %collective-permute-start.54 = (bf16[512,896]{1,0:T(8,128)(2,1)}, bf16[512,896]{1,0:T(8,128)(2,1)S(1)}, u32[]{:S(2)}, u32[]{:S(2)}) collective-permute-start(bf16[512,896]{1,0:T(8,128)(2,1)} %collective-permute-done.52.c_ref), channel_id=1, source_target_pairs={{0,8},{8,0},{16,24},{24,16},{1,9},{9,1},{17,25},{25,17},{2,10},{10... | collective-permute-start | bytes 2752520 | tf_op jit(solution)/shard_map/ppermute | solution.py:378
  272.5 231.5 %collective-permute-start.57 = (bf16[512,896]{1,0:T(8,128)(2,1)}, bf16[512,896]{1,0:T(8,128)(2,1)S(1)}, u32[]{:S(2)}, u32[]{:S(2)}) collective-permute-start(bf16[512,896]{1,0:T(8,128)(2,1)} %get-tuple-element.41), channel_id=1, source_target_pairs={{0,8},{8,0},{16,24},{24,16},{1,9},{9,1},{17,25},{25,17},{2,10},{10... | collective-permute-start | bytes 2752520 | tf_op jit(solution)/shard_map/ppermute | solution.py:378
  305.2 154.2 %collective-permute-start.58 = (bf16[512,896]{1,0:T(8,128)(2,1)}, bf16[512,896]{1,0:T(8,128)(2,1)S(1)}, u32[]{:S(2)}, u32[]{:S(2)}) collective-permute-start(bf16[512,896]{1,0:T(8,128)(2,1)} %get-tuple-element.43), channel_id=1, source_target_pairs={{0,8},{8,0},{16,24},{24,16},{1,9},{9,1},{17,25},{25,17},{2,10},{10... | collective-permute-start | bytes 2752520 | tf_op jit(solution)/shard_map/ppermute | solution.py:378
  305.2 154.5 %collective-permute-start.55 = (bf16[512,896]{1,0:T(8,128)(2,1)}, bf16[512,896]{1,0:T(8,128)(2,1)S(1)}, u32[]{:S(2)}, u32[]{:S(2)}) collective-permute-start(bf16[512,896]{1,0:T(8,128)(2,1)} %get-tuple-element.39), channel_id=1, source_target_pairs={{0,8},{8,0},{16,24},{24,16},{1,9},{9,1},{17,25},{25,17},{2,10},{10... | collective-permute-start | bytes 2752520 | tf_op jit(solution)/shard_map/ppermute | solution.py:378
  314.0 37.0 %collective-permute-start.78 = (bf16[112,640]{1,0:T(8,128)(2,1)S(1)}, bf16[112,640]{1,0:T(8,128)(2,1)S(1)}, u32[]{:S(2)}, u32[]{:S(2)}) collective-permute-start(bf16[112,640]{1,0:T(8,128)(2,1)S(1)} %get-tuple-element.141), channel_id=1, source_target_pairs={{0,1},{1,3},{3,5},{5,7},{7,6},{6,4},{4,2},{2,0},{8,9},{9,11},{11,1... | collective-permute-start | bytes 430088 | tf_op jit(solution)/shard_map/ppermute | solution.py:327
  325.3 36.1 %collective-permute-start.82 = (bf16[112,640]{1,0:T(8,128)(2,1)S(1)}, bf16[112,640]{1,0:T(8,128)(2,1)S(1)}, u32[]{:S(2)}, u32[]{:S(2)}) collective-permute-start(bf16[112,640]{1,0:T(8,128)(2,1)S(1)} %get-tuple-element.143), channel_id=1, source_target_pairs={{1,0},{3,1},{5,3},{7,5},{6,7},{4,6},{2,4},{0,2},{9,8},{11,9},{13,1... | collective-permute-start | bytes 430088 | tf_op jit(solution)/shard_map/ppermute | solution.py:327
  449.8 56.2 %collective-permute-start.50 = (bf16[512,896]{1,0:T(8,128)(2,1)S(1)}, bf16[512,896]{1,0:T(8,128)(2,1)S(1)}, u32[]{:S(2)}, u32[]{:S(2)}) collective-permute-start(bf16[512,896]{1,0:T(8,128)(2,1)S(1)} %copy-done.36), channel_id=1, source_target_pairs={{0,8},{8,0},{16,24},{24,16},{1,9},{9,1},{17,25},{25,17},{2,10},{10... | collective-permute-start | bytes 2752520 | tf_op jit(solution)/shard_map/ppermute | solution.py:378
  502.4 68.4 %collective-permute-start.87 = (bf16[112,1280]{1,0:T(8,128)(2,1)S(1)}, bf16[112,1280]{1,0:T(8,128)(2,1)}, u32[]{:S(2)}, u32[]{:S(2)}) collective-permute-start(bf16[112,1280]{1,0:T(8,128)(2,1)S(1)} %get-tuple-element.104), channel_id=1, source_target_pairs={{0,16},{8,24},{16,0},{24,8},{1,17},{9,25},{17,1},{25,9},{2,18},{10... | collective-permute-start | bytes 860168 | tf_op jit(solution)/shard_map/ppermute | solution.py:378
  504.0 78.2 %collective-permute-start.98 = (bf16[112,1280]{1,0:T(8,128)(2,1)}, bf16[112,1280]{1,0:T(8,128)(2,1)}, u32[]{:S(2)}, u32[]{:S(2)}) collective-permute-start(bf16[112,1280]{1,0:T(8,128)(2,1)} %get-tuple-element.102), channel_id=1, source_target_pairs={{0,16},{8,24},{16,0},{24,8},{1,17},{9,25},{17,1},{25,9},{2,18},{10... | collective-permute-start | bytes 860168 | tf_op jit(solution)/shard_map/ppermute | solution.py:378
  505.2 138.6 %collective-permute-start.108 = (bf16[112,1280]{1,0:T(8,128)(2,1)S(1)}, bf16[112,1280]{1,0:T(8,128)(2,1)}, u32[]{:S(2)}, u32[]{:S(2)}) collective-permute-start(bf16[112,1280]{1,0:T(8,128)(2,1)S(1)} %get-tuple-element.100), channel_id=1, source_target_pairs={{0,8},{8,0},{16,24},{24,16},{1,9},{9,1},{17,25},{25,17},{2,10},{10... | collective-permute-start | bytes 860168 | tf_op jit(solution)/shard_map/ppermute | solution.py:378
  506.0 76.3 %collective-permute-start.109 = (bf16[112,1280]{1,0:T(8,128)(2,1)S(1)}, bf16[112,1280]{1,0:T(8,128)(2,1)}, u32[]{:S(2)}, u32[]{:S(2)}) collective-permute-start(bf16[112,1280]{1,0:T(8,128)(2,1)S(1)} %get-tuple-element.100), channel_id=1, source_target_pairs={{0,16},{8,24},{16,0},{24,8},{1,17},{9,25},{17,1},{25,9},{2,18},{10... | collective-permute-start | bytes 860168 | tf_op jit(solution)/shard_map/ppermute | solution.py:378
  582.3 112.8 %collective-permute-start.88 = (bf16[112,1280]{1,0:T(8,128)(2,1)}, bf16[112,1280]{1,0:T(8,128)(2,1)S(1)}, u32[]{:S(2)}, u32[]{:S(2)}) collective-permute-start(bf16[112,1280]{1,0:T(8,128)(2,1)} %collective-permute-done.87), channel_id=1, source_target_pairs={{0,8},{8,0},{16,24},{24,16},{1,9},{9,1},{17,25},{25,17},{2,10},{10... | collective-permute-start | bytes 860168 | tf_op jit(solution)/shard_map/ppermute | solution.py:378
  582.3 126.2 %collective-permute-start.99 = (bf16[112,1280]{1,0:T(8,128)(2,1)}, bf16[112,1280]{1,0:T(8,128)(2,1)S(1)}, u32[]{:S(2)}, u32[]{:S(2)}) collective-permute-start(bf16[112,1280]{1,0:T(8,128)(2,1)} %collective-permute-done.98), channel_id=1, source_target_pairs={{0,8},{8,0},{16,24},{24,16},{1,9},{9,1},{17,25},{25,17},{2,10},{10... | collective-permute-start | bytes 860168 | tf_op jit(solution)/shard_map/ppermute | solution.py:378
  584.2 136.4 %collective-permute-start.110 = (bf16[112,1280]{1,0:T(8,128)(2,1)}, bf16[112,1280]{1,0:T(8,128)(2,1)S(1)}, u32[]{:S(2)}, u32[]{:S(2)}) collective-permute-start(bf16[112,1280]{1,0:T(8,128)(2,1)} %collective-permute-done.109), channel_id=1, source_target_pairs={{0,8},{8,0},{16,24},{24,16},{1,9},{9,1},{17,25},{25,17},{2,10},{10... | collective-permute-start | bytes 860168 | tf_op jit(solution)/shard_map/ppermute | solution.py:378
  739.6 45.2 %collective-permute-start.76 = (bf16[112,2048]{0,1:T(8,128)(2,1)S(1)}, bf16[112,2048]{0,1:T(8,128)(2,1)}, u32[]{:S(2)}, u32[]{:S(2)}) collective-permute-start(bf16[112,2048]{0,1:T(8,128)(2,1)S(1)} %add_convert_fusion.4), channel_id=1, source_target_pairs={{0,8},{8,0},{16,24},{24,16},{1,9},{9,1},{17,25},{25,17},{2,10},{10... | collective-permute-start | bytes 1376264 | tf_op jit(solution)/shard_map/ppermute | solution.py:378
  (132 other events, 1817.8 us)
